TPU v7x, 256 devices: a whole 4x4x8 slice. The times are simulated.
256 devices in a mesh: grp: 8 (over x_lo, y), shard: 32 (over x_hi, z, core).
Axes of the slice: x: 4 (x_hi: 2, x_lo: 2; x = x_hi * 2 + x_lo), y: 4, z: 8, core: 2. Of those that a mesh axis runs over, the one named last changes fastest.
Arguments:
- hidden_acts: bfloat16 [16384, 16384], P('shard', 'grp'), may hold values from -6 to 6
- cotangent: bfloat16 [16384, 5120], P('shard'), may hold values from -0.09375 to 0.09375
- master: float32 [5120, 16384], P('shard', 'grp'), may hold values from -0.046875 to 0.046875
- moment_one: float32 [5120, 16384], P('shard', 'grp'), may hold values from -3 to 3
- moment_two: float32 [5120, 16384], P('shard', 'grp'), may hold values from 0.01 to 1
- held_bucket: int32 [8], replicated, may hold values from 0 to 7, each once
- decode_in: bfloat16 [1024, 16384], P('grp', 'shard'), may hold values from -6 to 6
Outputs:
- master_new: float32 [5120, 16384], P('shard', 'grp')
- moment_one_new: float32 [5120, 16384], P('shard', 'grp')
- moment_two_new: float32 [5120, 16384], P('shard', 'grp')
- decode_out: bfloat16 [1024, 5120], P('grp', 'shard')
Inputs may be any that keep to these rules, and one draw needn't show every extreme that they name: held_bucket names each of the 8 buckets exactly once.
All inputs are finite; a program needn't handle non-finite values.
Results may differ from a plain program's by a relative error of at most 0.025.
Values may be sent and summed in bfloat16 or wider, within the bound.
A program may use at most 256 MiB of HBM per device.

v0:
```python
import jax
import jax.numpy as jnp
from jax import lax
from jax.sharding import PartitionSpec as P

beta_one = 0.9
beta_two = 0.95
learn_rate = 0.001
decay_rate = 0.1
epsilon = 1e-08
correct_one = 1.0 - 0.9**50
correct_two = 1.0 - 0.95**50


def pick_entry(table, position):
    marks = jnp.arange(table.shape[0], dtype=jnp.int32) == position
    return jnp.sum(jnp.where(marks, table, 0))


def body(hidden_acts, cotangent, master, moment_one, moment_two, held_bucket, decode_in):
    feat_rows = master.shape[0]
    bucket_cols = master.shape[1]
    gradient = lax.psum_scatter(
        lax.dot_general(
            cotangent, hidden_acts, (((0,), (0,)), ((), ())), preferred_element_type=jnp.float32
        ).astype(jnp.bfloat16),
        "shard",
        scatter_dimension=0,
        tiled=True,
    ).astype(jnp.float32)
    moment_one_new = beta_one * moment_one + (1.0 - beta_one) * gradient
    moment_two_new = beta_two * moment_two + (1.0 - beta_two) * gradient * gradient
    update = moment_one_new / correct_one / (jnp.sqrt(moment_two_new / correct_two) + epsilon)
    master_new = master - learn_rate * (update + decay_rate * master)
    weights = master_new.astype(jnp.bfloat16)
    full_rows = lax.all_gather(decode_in, "shard", axis=1, tiled=True)
    row_count = full_rows.shape[0]
    piece = lax.all_gather(weights, "grp", axis=1, tiled=True)
    buckets_here = piece.shape[1] // bucket_cols

    def one_bucket(offset, inner):
        bucket = pick_entry(held_bucket, offset)
        inputs = lax.dynamic_slice_in_dim(full_rows, bucket * bucket_cols, bucket_cols, 1)
        block_w = lax.dynamic_slice_in_dim(piece, offset * bucket_cols, bucket_cols, 1)
        return inner + lax.dot_general(
            inputs, block_w, (((1,), (1,)), ((), ())), preferred_element_type=jnp.float32
        )

    decode_sum = lax.fori_loop(
        0, buckets_here, one_bucket, jnp.zeros((row_count, feat_rows), jnp.float32)
    )
    return (master_new, moment_one_new, moment_two_new, decode_sum.astype(jnp.bfloat16))


def solution(mesh):
    placed = (
        P("shard", "grp"),
        P("shard", None),
        P("shard", "grp"),
        P("shard", "grp"),
        P("shard", "grp"),
        P(),
        P("grp", "shard"),
    )
    return jax.shard_map(
        body,
        mesh=mesh,
        in_specs=placed,
        out_specs=(P("shard", "grp"), P("shard", "grp"), P("shard", "grp"), P("grp", "shard")),
        check_vma=False,
    )
```

profile of v0, /device:TPU:24, one launch (start us, length us, event | category | flops | bytes accessed | tf_op | source)
XLA Modules:
  0.0 455.8 jit_solution(10346888529913700833)
XLA Ops:
  7.2 0.0 copy-start
  7.2 0.0 reduce-scatter.2.cloned.1.call-start
  7.2 1.5 copy-done
  8.8 16.6 %convolution_convert_fusion = bf16[5120,2048]{1,0:T(8,128)(2,1)} fusion(bf16[512,5120]{1,0:T(8,128)(2,1)} %param.10, bf16[512,2048]{1,0:T(8,128)(2,1)S(1)} %copy-done), kind=kOutput, calls=%fused_computation.6 | convolution fusion | flops 10747904000 | bytes 28311552 | tf_op jit(solution)/shard_map/dot_general | solution.py:24
  25.3 0.0 copy-start.1
  25.3 0.0 reduce-scatter.2.cloned.1.call-update
  25.4 0.0 all-gather.3.cloned.1.call-start
  25.4 0.7 all-gather.3.cloned.1.call-update
  26.1 0.0 copy-start.2
  26.1 0.0 all-gather.5.cloned.1.call-start
  26.2 248.6 %reduce-scatter.2.cloned.1.call-done = bf16[160,2048]{1,0:T(8,128)(2,1)} async-done(((bf16[5120,2048]{1,0:T(8,128)(2,1)}), bf16[160,2048]{1,0:T(8,128)(2,1)}) %reduce-scatter.2.cloned.1.call-update) | async-done | bytes 655376 | tf_op jit(solution)/shard_map/reduce_scatter | solution.py:23
  274.8 0.0 copy-done.1
  274.8 4.8 %fusion.6 = (bf16[160,2048]{1,0:T(8,128)(2,1)}, f32[160,2048]{1,0:T(8,128)}, f32[160,2048]{1,0:T(8,128)}, f32[160,2048]{1,0:T(8,128)}) fusion(f32[160,2048]{1,0:T(8,128)S(1)} %copy-done.1, bf16[160,2048]{1,0:T(8,128)(2,1)} %reduce-scatter.2.cloned.1.call-done, f32[160,2048]{1,0:T(8,128)} %param.12, f32[160,2048]{1,0:T(8,128)} %param.13), kind=kLoop, calls=%fused_computation.12 | loop fusion | flops 5570560 | bytes 9175040 | tf_op jit(solution)/shard_map/convert_element_type | solution.py:35
  279.5 0.0 all-gather.5.cloned.1.call-update
  279.6 83.1 %all-gather.3.cloned.1.call-done = bf16[128,16384]{1,0:T(8,128)(2,1)} async-done(((bf16[128,512]{1,0:T(8,128)(2,1)}), bf16[128,16384]{1,0:T(8,128)(2,1)}) %all-gather.3.cloned.1.call-update) | async-done | bytes 4194320 | tf_op jit(solution)/shard_map/all_gather | solution.py:36
  362.7 61.5 %all-gather.5.cloned.1.call-done = bf16[160,16384]{1,0:T(8,128)(2,1)} async-done(((bf16[160,2048]{1,0:T(8,128)(2,1)}), bf16[160,16384]{1,0:T(8,128)(2,1)}) %all-gather.5.cloned.1.call-update) | async-done | bytes 5242896 | tf_op jit(solution)/shard_map/all_gather | solution.py:38
  424.2 0.0 copy-done.2
  424.2 24.4 %while.14 = (s32[]{:T(128)}, f32[128,160]{0,1:T(8,128)S(1)}, s32[8]{0:T(128)S(1)}, bf16[128,16384]{1,0:T(8,128)(2,1)}, bf16[160,16384]{1,0:T(8,128)(2,1)}, /*index=5*/s32[]{:T(128)}, s32[]{:T(128)}, s32[]{:T(128)}, s32[]{:T(128)}) while((s32[]{:T(128)}, f32[128,160]{0,1:T(8,128)S(1)}, s32[8]{0:T(128)S(1)}, ...), condition=%wide.region_3.4_spmd.clone, body=%wide.region_1.3_spmd.clone.sunk | while | flops 83927072 | bytes 1343731 | solution.py:49
  424.2 0.7 fusion.16
  425.6 1.6 convolution_add_fusion.2
  427.2 0.7 fusion.16
  428.7 1.6 convolution_add_fusion.2
  430.3 0.7 fusion.16
  431.7 1.6 convolution_add_fusion.2
  433.4 0.7 fusion.16
  434.8 1.6 convolution_add_fusion.2
  436.4 0.7 fusion.16
  437.8 1.6 convolution_add_fusion.2
  439.5 0.7 fusion.16
  440.9 1.6 convolution_add_fusion.2
  442.5 0.7 fusion.16
  444.0 1.6 convolution_add_fusion.2
  445.6 0.7 fusion.16
  447.0 1.6 convolution_add_fusion.2
  448.6 0.6 convert_element_type.15
  (1 shorter events, 0.0 us)
Async XLA Ops:
  7.2 1.6 copy-start
  7.2 267.6 %reduce-scatter.2.cloned.1.call-start = ((), (), s32[]{:S(2)}) async-start(), calls=%async_computation.1 | async-start | bytes 21626880 | tf_op jit(solution)/shard_map/reduce_scatter | solution.py:23
  25.3 249.4 %copy-start.1 = (f32[160,2048]{1,0:T(8,128)S(1)}, f32[160,2048]{1,0:T(8,128)}, u32[]{:S(2)}) copy-start(f32[160,2048]{1,0:T(8,128)} %param.11) | copy-start | bytes 3932164
  25.4 337.3 %all-gather.3.cloned.1.call-start = ((), (), s32[]{:S(2)}) async-start(), calls=%async_computation.2 | async-start | bytes 4325376 | tf_op jit(solution)/shard_map/all_gather | solution.py:36
  26.1 398.1 %copy-start.2 = (s32[8]{0:T(128)S(1)}, s32[8]{0:T(128)}, u32[]{:S(2)}) copy-start(s32[8]{0:T(128)} %param.14) | copy-start | bytes 100
  26.1 398.1 %all-gather.5.cloned.1.call-start = ((), (), s32[]{:S(2)}) async-start(), calls=%async_computation.3 | async-start | bytes 5898240 | tf_op jit(solution)/shard_map/all_gather | solution.py:38
Sparse Core Ops, SparseCore 0:
  25.5 249.2 reduce-scatter.1
  277.6 85.0 all-gather.2
  364.6 59.5 all-gather.4
where the time goes:
time: 460 us; the launch traced here: 456 us
  waiting for transfers between devices  394 us (86%)
  matrix products  29.4 us (6%)
  between operations  13.8 us (3%)
  other arithmetic  11.1 us (2%)
  loops' own time  5.87 us (1%)
    reduce_scatter x1, waiting for transfers between devices, body(): lax.psum_scatter(lax.dot_general(cotangent, hidden_acts, (((0,), (0,)), (...  249 us
    all_gather x1, waiting for transfers between devices, body(): full_rows = lax.all_gather(decode_in, 'shard', axis=1, tiled=True)  83.1 us
    all_gather x1, waiting for transfers between devices, body(): piece = lax.all_gather(weights, 'grp', axis=1, tiled=True)  61.5 us
    dot_general x1, matrix products, body(): lax.dot_general(cotangent, hidden_acts, (((0,), (0,)), ((), ())), preferr...  16.6 us
    dot_general x8, matrix products, one_bucket(): lax.dot_general(inputs, block_w, (((1,), (1,)), ((), ())), preferred_elem...  12.8 us
  transfers between devices with their start and end apart: 3, of which 3 were waited for; matrix products, arithmetic and copies ran while one was open for 1% of the time, Pallas kernels for 0%

commit v1 on v0

v1 whole, which is shorter than its diff:
```python
import jax
import jax.numpy as jnp
from jax import lax
from jax.experimental import pallas as pl
from jax.experimental.pallas import tpu as pltpu
from jax.sharding import PartitionSpec as P

beta_one = 0.9
beta_two = 0.95
learn_rate = 0.001
decay_rate = 0.1
epsilon = 1e-08
correct_one = 1.0 - 0.9**50
correct_two = 1.0 - 0.95**50

NX, NY, NZ = 4, 4, 8
FEAT = 5120
HALF = FEAT // 2
OWN = 160
CHIP = 2 * OWN
TOK = 512
BUCKET = 2048
COLS = BUCKET // 2
WAVES = 4
WCOL = COLS // WAVES
LANE = WCOL // 2
PIECES = 4
PCOL = HALF // PIECES
PROW = TOK // NY
ROWS = 128
DCOL = 512
LAG = 2
LAST = 11


def aligned(value, step):
    return pl.multiple_of(value, step)


def device_at(x, y, z, core):
    x, y, z = lax.rem(x, NX), lax.rem(y, NY), lax.rem(z, NZ)
    return {
        "grp": lax.rem(x, 2) * NY + y,
        "shard": (x // 2) * 16 + z * 2 + core,
    }


def kernel(
    hid, cot, master, mom_one, mom_two, held, dec,
    master_out, one_out, two_out, dec_out,
    cotv, hidv, pv, rv, gx, st, wv, xv, acc,
    local_sem, in_send, in_recv,
    cc_send, cc_recv, cy_send, cy_recv, cf_send, cf_recv, cs_send, cs_recv,
    hx_send, hx_recv, xx_send, xx_recv, xz_send, xz_recv, xs_send, xs_recv,
    r_send, r_recv, g_send, g_recv,
    ax_send, ax_recv, ay_send, ay_recv, af_send, af_recv, out_sem,
):
    grp = lax.axis_index("grp")
    shard = lax.axis_index("shard")
    x_lo, y = grp // NY, lax.rem(grp, NY)
    x_hi, z, core = shard // 16, lax.rem(shard, 16) // 2, lax.rem(shard, 2)
    x = x_hi * 2 + x_lo
    other = 1 - core

    sibling = device_at(x, y, z, other)
    z_up, z_down = device_at(x, y, z + 1, core), device_at(x, y, z + NZ - 1, core)
    y_up, y_down = device_at(x, y + 1, z, core), device_at(x, y + NY - 1, z, core)
    x_half = device_at(x + 2, y, z, core)
    x_half_other = device_at(x + 2, y, z, other)
    x_cross = device_at(3 - x, y, z, core)
    x_pair = device_at(x_hi * 2 + 1 - x_lo, y, z, core)
    z_way = (z_up, z_down)
    y_way = (y_up, y_down)

    def remote(src, dst, send, recv, device):
        return pltpu.make_async_remote_copy(
            src_ref=src, dst_ref=dst, send_sem=send, recv_sem=recv,
            device_id=device, device_id_type=pl.DeviceIdType.MESH,
        )

    barrier = pltpu.get_barrier_semaphore()
    partners = (
        sibling, z_up, z_down, y_up, y_down, x_half, x_half_other, x_cross, x_pair,
    )
    for partner in partners:
        pl.semaphore_signal(
            barrier, inc=1, device_id=partner, device_id_type=pl.DeviceIdType.MESH
        )

    mine = pl.ds(aligned(core * TOK, TOK), TOK)
    loads = [
        pltpu.make_async_copy(
            cot.at[:, pl.ds(aligned(x_hi * HALF, HALF), HALF)], cotv.at[mine, :],
            local_sem.at[0],
        ),
        pltpu.make_async_copy(
            hid.at[:, pl.ds(aligned(core * COLS, COLS), COLS)], hidv.at[mine, :],
            local_sem.at[1],
        ),
        pltpu.make_async_copy(
            dec, xv.at[shard], local_sem.at[2]
        ),
        pltpu.make_async_copy(master, st.at[0], local_sem.at[3]),
        pltpu.make_async_copy(mom_one, st.at[1], local_sem.at[4]),
        pltpu.make_async_copy(mom_two, st.at[2], local_sem.at[5]),
    ]
    for copy in loads:
        copy.start()

    def cot_sibling():
        return remote(
            cot.at[:, pl.ds(aligned(x_hi * HALF, HALF), HALF)], cotv.at[mine, :],
            in_send.at[0], in_recv.at[0], sibling,
        )

    def hid_sibling():
        return remote(
            hid.at[:, pl.ds(aligned(other * COLS, COLS), COLS)], hidv.at[mine, :],
            in_send.at[1], in_recv.at[1], sibling,
        )

    def cot_rows(owner, first, count):
        return pl.ds(aligned((2 + core) * TOK + owner * PROW + first, 64), count)

    def cot_cols(piece):
        return pl.ds(aligned(piece * PCOL, PCOL), PCOL)

    def cot_cross(piece):
        return remote(
            cot.at[
                pl.ds(aligned(y * PROW, PROW), PROW),
                pl.ds(aligned((1 - x_hi) * HALF + piece * PCOL, 128), PCOL),
            ],
            cotv.at[cot_rows(y, 0, PROW), cot_cols(piece)],
            cc_send.at[piece], cc_recv.at[piece], x_cross,
        )

    def cot_y(way, piece):
        part = cotv.at[cot_rows(y, 0, PROW), cot_cols(piece)]
        return remote(
            part, part, cy_send.at[way, piece], cy_recv.at[way, piece], y_way[way]
        )

    def cot_forward(way, piece):
        owner = lax.rem(y + (NY - 1 if way == 0 else 1), NY)
        part = cotv.at[cot_rows(owner, way * (PROW // 2), PROW // 2), cot_cols(piece)]
        return remote(
            part, part, cf_send.at[way, piece], cf_recv.at[way, piece], y_way[way]
        )

    def cot_share(which, piece):
        owner = lax.rem(y + (0, NY - 1, 1, 2)[which], NY)
        part = cotv.at[cot_rows(owner, 0, PROW), cot_cols(piece)]
        return remote(
            part, part, cs_send.at[which, piece], cs_recv.at[which, piece], sibling
        )

    def wave_cols(wave):
        return pl.ds(aligned(wave * WCOL, WCOL), WCOL)

    def hid_half(wave, target):
        rows = pl.ds(aligned((2 + core) * TOK, TOK), TOK)
        device = device_at(x + 2, y, z, target)
        return remote(
            hid.at[:, pl.ds(aligned(target * COLS + wave * WCOL, WCOL), WCOL)],
            hidv.at[rows, wave_cols(wave)],
            hx_send.at[wave, target], hx_recv.at[wave, core], device,
        )

    def hid_half_wait(wave, source):
        part = hidv.at[pl.ds((2 + source) * TOK, TOK), wave_cols(wave)]
        pltpu.make_async_copy(part, part, hx_recv.at[wave, source]).wait()

    def dec_index(half, place):
        return half * 16 + place * 2 + core

    def dec_half():
        return remote(
            dec, xv.at[shard],
            xx_send.at[0], xx_recv.at[0], x_half,
        )

    def dec_z(part, way, step):
        half = x_hi if part == 0 else 1 - x_hi
        place = lax.rem(z + (NZ - step if way == 0 else step), NZ)
        rows = pl.ds(0, ROWS)
        if step == 3:
            rows = pl.ds(way * (ROWS // 2), ROWS // 2)
        block = xv.at[dec_index(half, place), rows]
        return remote(
            block, block, xz_send.at[part, way, step], xz_recv.at[part, way, step],
            z_way[way],
        )

    def dec_share(part, slot):
        half = x_hi if part == 0 else 1 - x_hi
        shift = (NZ - 1, NZ - 2, NZ - 3, 1, 2, 3, 4, 0)[slot]
        block = xv.at[dec_index(half, lax.rem(z + shift, NZ))]
        return remote(
            block, block, xs_send.at[part, slot], xs_recv.at[part, slot], sibling
        )

    def ring_block(way, step):
        if way == 0:
            return lax.rem(z + 2 * NZ - 1 - step, NZ)
        return lax.rem(z + 1 + step, NZ)

    def ring_rows(place):
        return pl.ds(aligned(place * CHIP, CHIP), CHIP)

    def ring_first(wave, way):
        return remote(
            pv.at[wave, ring_rows(ring_block(way, 0)), pl.ds(way * LANE, LANE)],
            rv.at[wave, way, 0],
            r_send.at[wave, way, 0], r_recv.at[wave, way, 0], z_way[way],
        )

    def ring_next(wave, way, step):
        return remote(
            rv.at[wave, way, step - 1], rv.at[wave, way, step],
            r_send.at[wave, way, step], r_recv.at[wave, way, step], z_way[way],
        )

    def chip_rows(which):
        return pl.ds(aligned(z * CHIP + which * OWN, 32), OWN)

    def grad_swap(wave):
        return remote(
            pv.at[wave, chip_rows(other), :], gx.at[wave],
            g_send.at[wave], g_recv.at[wave], sibling,
        )

    def weights_pair(wave):
        block = wv.at[grp, wave]
        return remote(block, block, ax_send.at[wave], ax_recv.at[wave], x_pair)

    def weights_y(wave, part, way):
        side = x_lo if part == 0 else 1 - x_lo
        block = wv.at[side * NY + y, wave]
        return remote(
            block, block, ay_send.at[wave, part, way], ay_recv.at[wave, part, way],
            y_way[way],
        )

    def weights_forward(wave, part, way):
        side = x_lo if part == 0 else 1 - x_lo
        owner = lax.rem(y + (NY - 1 if way == 0 else 1), NY)
        block = wv.at[side * NY + owner, wave, pl.ds(way * (OWN // 2), OWN // 2), :]
        return remote(
            block, block, af_send.at[wave, part, way], af_recv.at[wave, part, way],
            y_way[way],
        )

    def state_cols(wave, half):
        return pl.ds(aligned(half * COLS + wave * WCOL, WCOL), WCOL)

    def store_out(wave, half, which):
        cols = state_cols(wave, half)
        target = (master_out, one_out, two_out)[which]
        return pltpu.make_async_copy(
            st.at[which, :, cols], target.at[:, cols], out_sem.at[wave, half, which]
        )

    pl.semaphore_wait(barrier, len(partners))
    for piece in range(PIECES):
        cot_cross(piece).start()
    dec_half().start()
    loads[2].wait()
    for way in range(2):
        dec_z(0, way, 0).start()
    dec_share(0, 7).start()
    cot_sibling().start()
    hid_sibling().start()

    for piece in range(PIECES):
        cot_cross(piece).wait_recv()
        for way in range(2):
            cot_y(way, piece).start()
        cot_share(0, piece).start()
        if piece == 0:
            dec_half().wait_recv()
            for way in range(2):
                dec_z(1, way, 0).start()
            dec_share(1, 7).start()
        if piece == 1:
            for target in range(2):
                hid_half(0, target).start()
    for wave in range(1, WAVES):
        for target in range(2):
            hid_half(wave, target).start()

    for piece in range(PIECES):
        for way in range(2):
            cot_y(way, piece).wait_recv()
            cot_forward(way, piece).start()
            cot_share(1 + way, piece).start()
        if piece < 3:
            for part in range(2):
                for way in range(2):
                    dec_z(part, way, piece).wait_recv()
                    dec_z(part, way, piece + 1).start()
                    dec_share(part, way * 3 + piece).start()
    for piece in range(PIECES):
        for way in range(2):
            cot_forward(way, piece).wait_recv()
        cot_share(3, piece).start()
    for part in range(2):
        for way in range(2):
            dec_z(part, way, 3).wait_recv()
        dec_share(part, 6).start()

    acc[...] = jnp.zeros_like(acc)
    loads[0].wait()
    loads[1].wait()
    for which in range(3):
        loads[3 + which].wait()
    cot_sibling().wait_recv()
    hid_sibling().wait_recv()
    for which in range(4):
        for piece in range(PIECES):
            cot_share(which, piece).wait_recv()
    for part in range(2):
        for slot in range(8):
            dec_share(part, slot).wait_recv()

    def stage_sum(wave):
        for source in range(2):
            hid_half_wait(wave, source)

        def tile(index, carry):
            cols = pl.ds(aligned(index * PCOL, PCOL), PCOL)
            value = lax.dot_general(
                cotv[:, cols], hidv[:, wave_cols(wave)],
                (((0,), (0,)), ((), ())), preferred_element_type=jnp.float32,
            )
            pv[wave, cols, :] = value.astype(jnp.bfloat16)
            return carry

        lax.fori_loop(0, PIECES, tile, 0)
        for way in range(2):
            ring_first(wave, way).start()

    def stage_ring(wave, step):
        for way in range(2):
            pltpu.make_async_copy(
                rv.at[wave, way, step - 1], rv.at[wave, way, step - 1],
                r_recv.at[wave, way, step - 1],
            ).wait()
            own = pv[wave, ring_rows(ring_block(way, step)), way * LANE:(way + 1) * LANE]
            total = rv[wave, way, step - 1].astype(jnp.float32) + own.astype(jnp.float32)
            rv[wave, way, step - 1] = total.astype(jnp.bfloat16)
            ring_next(wave, way, step).start()

    def stage_home(wave):
        step = NZ - 1
        for way in range(2):
            pltpu.make_async_copy(
                rv.at[wave, way, step - 1], rv.at[wave, way, step - 1],
                r_recv.at[wave, way, step - 1],
            ).wait()
            lanes = slice(way * LANE, (way + 1) * LANE)
            own = pv[wave, ring_rows(z), lanes]
            total = rv[wave, way, step - 1].astype(jnp.float32) + own.astype(jnp.float32)
            pv[wave, ring_rows(z), lanes] = total.astype(jnp.bfloat16)
        grad_swap(wave).start()

    def adamw(wave, half, gradient):
        cols = state_cols(wave, half)
        master_now = st[0, :, cols]
        one = beta_one * st[1, :, cols] + (1.0 - beta_one) * gradient
        two = beta_two * st[2, :, cols] + (1.0 - beta_two) * gradient * gradient
        update = one / correct_one / (jnp.sqrt(two / correct_two) + epsilon)
        fresh = master_now - learn_rate * (update + decay_rate * master_now)
        st[0, :, cols] = fresh
        st[1, :, cols] = one
        st[2, :, cols] = two
        wv[grp, wave, :, pl.ds(aligned(half * WCOL, WCOL), WCOL)] = fresh.astype(jnp.bfloat16)

    def stage_update(wave):
        adamw(wave, core, pv[wave, chip_rows(core), :].astype(jnp.float32))
        grad_swap(wave).wait_recv()
        adamw(wave, other, gx[wave].astype(jnp.float32))
        weights_pair(wave).start()
        for way in range(2):
            weights_y(wave, 0, way).start()
        for half in range(2):
            for which in range(3):
                store_out(wave, half, which).start()

    def stage_spread(wave):
        weights_pair(wave).wait_recv()
        for way in range(2):
            weights_y(wave, 1, way).start()
        for way in range(2):
            weights_y(wave, 0, way).wait_recv()
            weights_forward(wave, 0, way).start()

    def stage_far(wave):
        for way in range(2):
            weights_y(wave, 1, way).wait_recv()
            weights_forward(wave, 1, way).start()

    def stage_decode(wave):
        for part in range(2):
            for way in range(2):
                weights_forward(wave, part, way).wait_recv()

        lanes = pl.ds(aligned(lax.rem(wave, 2) * WCOL, WCOL), WCOL)

        def bucket_step(index, total):
            first = held[index] * 4 + wave // 2
            for half in range(2):
                total = total + lax.dot_general(
                    xv[first + 2 * half, :, lanes],
                    wv[index, wave, :, half * WCOL:(half + 1) * WCOL],
                    (((1,), (1,)), ((), ())), preferred_element_type=jnp.float32,
                )
            return total

        acc[...] = lax.fori_loop(0, 8, bucket_step, acc[...])

    def tick(now, carry):
        def each(wave, inner):
            stage = now - LAG * wave
            pl.when(stage == 0)(lambda: stage_sum(wave))
            pl.when(jnp.logical_and(stage >= 1, stage <= 6))(
                lambda: stage_ring(wave, stage)
            )
            pl.when(stage == 7)(lambda: stage_home(wave))
            pl.when(stage == 8)(lambda: stage_update(wave))
            pl.when(stage == 9)(lambda: stage_spread(wave))
            pl.when(stage == 10)(lambda: stage_far(wave))
            pl.when(stage == LAST)(lambda: stage_decode(wave))
            return inner

        return lax.fori_loop(0, WAVES, each, carry)

    lax.fori_loop(0, LAST + 1 + LAG * (WAVES - 1), tick, 0)
    dec_out[...] = acc[...].astype(jnp.bfloat16)

    cot_sibling().wait_send()
    hid_sibling().wait_send()
    dec_half().wait_send()
    for piece in range(PIECES):
        cot_cross(piece).wait_send()
        for way in range(2):
            cot_y(way, piece).wait_send()
            cot_forward(way, piece).wait_send()
        for which in range(4):
            cot_share(which, piece).wait_send()
    for part in range(2):
        for way in range(2):
            for step in range(4):
                dec_z(part, way, step).wait_send()
        for slot in range(8):
            dec_share(part, slot).wait_send()

    def drain(wave, carry):
        for target in range(2):
            hid_half(wave, target).wait_send()
        for way in range(2):
            ring_first(wave, way).wait_send()
            for step in range(1, NZ - 1):
                ring_next(wave, way, step).wait_send()
        grad_swap(wave).wait_send()
        weights_pair(wave).wait_send()
        for part in range(2):
            for way in range(2):
                weights_y(wave, part, way).wait_send()
                weights_forward(wave, part, way).wait_send()
        for half in range(2):
            for which in range(3):
                store_out(wave, half, which).wait()
        return carry

    lax.fori_loop(0, WAVES, drain, 0)


def body(hidden_acts, cotangent, master, moment_one, moment_two, held_bucket, decode_in):
    any_spec = pl.BlockSpec(memory_space=pl.ANY)
    vmem = pltpu.VMEM
    sems = pltpu.SemaphoreType.DMA
    bf16, f32 = jnp.bfloat16, jnp.float32
    state = jax.ShapeDtypeStruct((OWN, BUCKET), f32)
    steps = NZ - 1
    pairs = [
        (2,), (PIECES,), (2, PIECES), (2, PIECES), (4, PIECES), (WAVES, 2), (1,),
        (2, 2, 4), (2, 8), (WAVES, 2, steps), (WAVES,), (WAVES,), (WAVES, 2, 2),
        (WAVES, 2, 2),
    ]
    both = [sems(shape) for shape in pairs for _ in range(2)]
    return pl.pallas_call(
        kernel,
        out_shape=(state, state, state, jax.ShapeDtypeStruct((ROWS, OWN), bf16)),
        in_specs=[any_spec] * 5 + [pl.BlockSpec(memory_space=pltpu.SMEM), any_spec],
        out_specs=(any_spec, any_spec, any_spec, pl.BlockSpec(memory_space=pltpu.VMEM)),
        scratch_shapes=[
            vmem((4 * TOK, HALF), bf16),
            vmem((4 * TOK, COLS), bf16),
            vmem((WAVES, HALF, WCOL), bf16),
            vmem((WAVES, 2, steps, CHIP, LANE), bf16),
            vmem((WAVES, OWN, WCOL), bf16),
            vmem((3, OWN, BUCKET), f32),
            vmem((8, WAVES, OWN, 2 * WCOL), bf16),
            vmem((32, ROWS, DCOL), bf16),
            vmem((ROWS, OWN), f32),
            sems((6,)),
            *both,
            sems((WAVES, 2, 3)),
        ],
        compiler_params=pltpu.CompilerParams(
            collective_id=0, has_side_effects=True, vmem_limit_bytes=58 * 2**20
        ),
        cost_estimate=pl.CostEstimate(
            flops=12_000_000_000, bytes_accessed=30_000_000, transcendentals=0
        ),
    )(hidden_acts, cotangent, master, moment_one, moment_two, held_bucket, decode_in)


def solution(mesh):
    placed = (
        P("shard", "grp"),
        P("shard", None),
        P("shard", "grp"),
        P("shard", "grp"),
        P("shard", "grp"),
        P(),
        P("grp", "shard"),
    )
    return jax.shard_map(
        body,
        mesh=mesh,
        in_specs=placed,
        out_specs=(P("shard", "grp"), P("shard", "grp"), P("shard", "grp"), P("grp", "shard")),
        check_vma=False,
    )
```

time: 460 us -> 168 us (0.37)
  waiting for transfers between devices: 394 us -> 0 us
  Pallas kernels: 0 us -> 159 us
  matrix products: 29.4 us -> 0 us
  between operations: 13.8 us -> 0.64 us
  other arithmetic: 11.1 us -> 0 us
  loops' own time: 5.87 us -> 0 us
  local copies, waits for them, and re-layouts: 1.55 us -> 7.01 us
    reduce_scatter x1 -> x0, waiting for transfers between devices: 249 us -> none  [body(): lax.psum_scatter(lax.dot_general(cotangent, hidden_acts, (((0,), (0,)), (...]
    pallas_call x0 -> x1, Pallas kernels: none -> 159 us  [body(): pl.pallas_call(kernel, out_shape=(state, state, state, jax.ShapeDtypeStru...]
    all_gather x2 -> x0, waiting for transfers between devices: 145 us -> none  [the longest x1 83.1 us: body(): full_rows = lax.all_gather(decode_in, 'shard', axis=1, tiled=True)]
    dot_general x9 -> x0, matrix products: 29.4 us -> none  [the longest x1 16.6 us: body(): lax.dot_general(cotangent, hidden_acts, (((0,), (0,)), ((), ())), preferr...]
    another operation x1 -> x0, loops' own time: 5.87 us -> none  [body(): lax.fori_loop(0, buckets_here, one_bucket, jnp.zeros((row_count, feat_row...]
    reduce_sum x8 -> x0, other arithmetic: 5.72 us -> none  [pick_entry(): return jnp.sum(jnp.where(marks, table, 0))]
    convert_element_type x2 -> x0, other arithmetic: 5.4 us -> none  [the longest x1 4.78 us: body(): weights = master_new.astype(jnp.bfloat16)]
  transfers between devices with their start and end apart: 3 -> 0, of which waited for: 3 -> 0; matrix products, arithmetic and copies ran while one was open for 1% -> 0% of each run, Pallas kernels for 0% -> 0%
where the time goes in v1:
time: 168 us; the launch traced here: 166 us
  Pallas kernels  159 us (95%)
  local copies, waits for them, and re-layouts  7.01 us (4%)
    pallas_call x1, Pallas kernels, body(): pl.pallas_call(kernel, out_shape=(state, state, state, jax.ShapeDtypeStru...  159 us
    unnamed x7, local copies, waits for them, and re-layouts  5.45 us

profile of v1, /device:TPU:24, one launch (start us, length us, event | category | flops | bytes accessed | tf_op | source)
XLA Modules:
  0.0 166.3 jit_solution(11833022042438965194)
XLA Ops:
  0.6 158.6 %shard_map.102 = (f32[160,2048]{1,0:T(8,128)}, f32[160,2048]{1,0:T(8,128)}, f32[160,2048]{1,0:T(8,128)}, bf16[128,160]{1,0:T(8,128)(2,1)}) custom-call(bf16[512,2048]{1,0:T(8,128)(2,1)} %hid.1, bf16[512,5120]{1,0:T(8,128)(2,1)} %cot.1, f32[160,2048]{1,0:T(8,128)} %master.1, f32[160,2048]{1,0:T(8,128)} %mom_one.1, f32[160,2048]{1,0:T(8,128)} %mom_two.1, ...), custom_call_target="tpu_custom_call" | custom-call | flops 12000000000 | bytes 30000000 | tf_op jit(solution)/shard_map/pallas_call | solution.py:492
  159.2 1.6 copy.11
  160.8 0.0 copy-start.1
  160.8 2.6 %copy.15 = f32[160,2048]{1,0:T(8,128)} copy(f32[160,2048]{1,0:T(8,128)} %get-tuple-element.12) | data formatting | bytes 2621440
  163.4 0.0 copy-done.1
  163.4 0.0 copy-start
  163.4 1.1 copy.16
  164.5 0.7 copy-done
  165.2 1.1 copy.17
Async XLA Ops:
  160.8 2.6 %copy-start.1 = (f32[160,2048]{1,0:T(8,128)S(1)}, f32[160,2048]{1,0:T(8,128)}, u32[]{:S(2)}) copy-start(f32[160,2048]{1,0:T(8,128)} %get-tuple-element.13) | copy-start | bytes 3932164
  163.4 1.8 %copy-start = (f32[160,2048]{1,0:T(8,128)S(1)}, f32[160,2048]{1,0:T(8,128)}, u32[]{:S(2)}) copy-start(f32[160,2048]{1,0:T(8,128)} %get-tuple-element.14) | copy-start | bytes 3932164

commit v2 on v1

v2 whole, which is shorter than its diff:
```python
import jax
import jax.numpy as jnp
from jax import lax
from jax.experimental import pallas as pl
from jax.experimental.pallas import tpu as pltpu
from jax.sharding import PartitionSpec as P

beta_one = 0.9
beta_two = 0.95
learn_rate = 0.001
decay_rate = 0.1
epsilon = 1e-08
correct_one = 1.0 - 0.9**50
correct_two = 1.0 - 0.95**50

NX, NY, NZ = 4, 4, 8
FEAT = 5120
HALF = FEAT // 2
OWN = 160
CHIP = 2 * OWN
TOK = 512
BUCKET = 2048
COLS = BUCKET // 2
WAVES = 4
WCOL = COLS // WAVES
LANE = WCOL // 2
PIECES = 4
PCOL = HALF // PIECES
PROW = TOK // NY
ROWS = 128
DCOL = 512
RINGS = WAVES + 1
LAST = 14
GROUPS = 8
HROWS = ROWS // 2
SLICES = 16


def aligned(value, step):
    return pl.multiple_of(value, step)


def device_at(x, y, z, core):
    x, y, z = lax.rem(x, NX), lax.rem(y, NY), lax.rem(z, NZ)
    return {
        "grp": lax.rem(x, 2) * NY + y,
        "shard": (x // 2) * 16 + z * 2 + core,
    }


def kernel(
    hid, cot, master, mom_one, mom_two, held, dec,
    master_out, one_out, two_out, dec_out,
    cotv, cotx, hidv, pv, rv, gx, hx, st, wv, a2, pick, xv, acc, dsend, drecv,
    local_sem, a_recv, in_send, in_recv,
    cc_send, cc_recv, cy_send, cy_recv, cf_send, cf_recv, cs_send, cs_recv,
    hx_send, hx_recv, xx_send, xx_recv, xz_send, xz_recv, xs_send, xs_recv,
    r_send, r_recv, g_send, g_recv, h_send, h_recv, a_send, p_send, p_recv, d_send, d_recv, out_sem,
):
    grp = lax.axis_index("grp")
    shard = lax.axis_index("shard")
    x_lo, y = grp // NY, lax.rem(grp, NY)
    x_hi, z, core = shard // 16, lax.rem(shard, 16) // 2, lax.rem(shard, 2)
    x = x_hi * 2 + x_lo
    other = 1 - core

    sibling = device_at(x, y, z, other)
    z_up, z_down = device_at(x, y, z + 1, core), device_at(x, y, z + NZ - 1, core)
    y_up, y_down = device_at(x, y + 1, z, core), device_at(x, y + NY - 1, z, core)
    x_half = device_at(x + 2, y, z, core)
    x_half_other = device_at(x + 2, y, z, other)
    x_cross = device_at(3 - x, y, z, core)
    slot_here = shard // 2
    z_way = (z_up, z_down)
    y_way = (y_up, y_down)

    def remote(src, dst, send, recv, device):
        return pltpu.make_async_remote_copy(
            src_ref=src, dst_ref=dst, send_sem=send, recv_sem=recv,
            device_id=device, device_id_type=pl.DeviceIdType.MESH,
        )

    barrier = pltpu.get_barrier_semaphore()
    partners = (
        sibling, z_up, z_down, y_up, y_down, x_half, x_half_other, x_cross,
    )

    def greet(device):
        pl.semaphore_signal(
            barrier, inc=1, device_id=device, device_id_type=pl.DeviceIdType.MESH
        )

    def peer(offset):
        return {"grp": lax.rem(grp + offset, GROUPS), "shard": shard}

    for partner in partners:
        greet(partner)
    for offset in range(1, GROUPS):
        greet(peer(offset))
    for bucket in range(GROUPS):
        source = bucket * 4 + shard // 8

        @pl.when(source != shard)
        def _():
            greet({"grp": grp, "shard": source})

    keeps_one = jnp.where(lax.rem(shard, 4) == shard // 8, 1, 0)

    mine = pl.ds(aligned(core * TOK, TOK), TOK)
    loads = [
        pltpu.make_async_copy(
            cot.at[:, pl.ds(aligned(x_hi * HALF, HALF), HALF)], cotv.at[mine, :],
            local_sem.at[0],
        ),
        pltpu.make_async_copy(
            hid.at[:, pl.ds(aligned(core * COLS, COLS), COLS)], hidv.at[mine, :],
            local_sem.at[1],
        ),
        pltpu.make_async_copy(master, st.at[0], local_sem.at[2]),
        pltpu.make_async_copy(mom_one, st.at[1], local_sem.at[3]),
        pltpu.make_async_copy(mom_two, st.at[2], local_sem.at[4]),
        pltpu.make_async_copy(
            cot.at[:, pl.ds(aligned((1 - x_hi) * HALF, HALF), HALF)], cotx.at[mine, :],
            local_sem.at[5],
        ),
    ]
    for copy in loads:
        copy.start()

    def cot_sibling():
        return remote(
            cot.at[:, pl.ds(aligned(x_hi * HALF, HALF), HALF)], cotv.at[mine, :],
            in_send.at[0], in_recv.at[0], sibling,
        )

    def cotx_sibling():
        return remote(
            cot.at[:, pl.ds(aligned((1 - x_hi) * HALF, HALF), HALF)], cotx.at[mine, :],
            in_send.at[2], in_recv.at[2], sibling,
        )

    def hid_sibling():
        return remote(
            hid.at[:, pl.ds(aligned(other * COLS, COLS), COLS)], hidv.at[mine, :],
            in_send.at[1], in_recv.at[1], sibling,
        )

    def cot_rows(owner, first, count):
        return pl.ds(aligned((2 + core) * TOK + owner * PROW + first, 64), count)

    def cot_cols(piece):
        return pl.ds(aligned(piece * PCOL, PCOL), PCOL)

    def cot_cross(piece):
        return remote(
            cot.at[
                pl.ds(aligned(y * PROW, PROW), PROW),
                pl.ds(aligned((1 - x_hi) * HALF + piece * PCOL, 128), PCOL),
            ],
            cotv.at[cot_rows(y, 0, PROW), cot_cols(piece)],
            cc_send.at[piece], cc_recv.at[piece], x_cross,
        )

    def cot_y(way, piece):
        part = cotv.at[cot_rows(y, 0, PROW), cot_cols(piece)]
        return remote(
            part, part, cy_send.at[way, piece], cy_recv.at[way, piece], y_way[way]
        )

    def cot_forward(way, piece):
        owner = lax.rem(y + (NY - 1 if way == 0 else 1), NY)
        part = cotv.at[cot_rows(owner, way * (PROW // 2), PROW // 2), cot_cols(piece)]
        return remote(
            part, part, cf_send.at[way, piece], cf_recv.at[way, piece], y_way[way]
        )

    def cot_share(which, piece):
        owner = lax.rem(y + (0, NY - 1, 1, 2)[which], NY)
        part = cotv.at[cot_rows(owner, 0, PROW), cot_cols(piece)]
        return remote(
            part, part, cs_send.at[which, piece], cs_recv.at[which, piece], sibling
        )

    def wave_cols(wave):
        return pl.ds(aligned(wave * WCOL, WCOL), WCOL)

    def hid_half(wave, target):
        rows = pl.ds(aligned((2 + core) * TOK, TOK), TOK)
        device = device_at(x + 2, y, z, target)
        return remote(
            hid.at[:, pl.ds(aligned(target * COLS + wave * WCOL, WCOL), WCOL)],
            hidv.at[rows, wave_cols(wave)],
            hx_send.at[wave, target], hx_recv.at[wave, core], device,
        )

    def hid_half_wait(wave, source):
        part = hidv.at[pl.ds((2 + source) * TOK, TOK), wave_cols(wave)]
        pltpu.make_async_copy(part, part, hx_recv.at[wave, source]).wait()

    def dec_target(index, which):
        return (lax.rem(shard, 4) * 4 + index) * 2 + which

    def dec_slice(index, which):
        return dec.at[pl.ds(which * HROWS, HROWS), pl.ds(index * 128, 128)]

    def dec_away(index, which):
        return remote(
            dec_slice(index, which), a2.at[shard // 4],
            a_send.at[index, which], a_recv.at[shard // 4],
            {"grp": grp, "shard": dec_target(index, which)},
        )

    def dec_here(index, which):
        return pltpu.make_async_copy(
            dec_slice(index, which), a2.at[shard // 4], a_recv.at[shard // 4]
        )

    def dec_pick(offset):
        return remote(
            pick.at[lax.rem(grp + offset, GROUPS)], xv.at[slot_here, core, grp],
            p_send.at[offset], p_recv.at[offset], peer(offset),
        )

    def dec_index(half, place):
        return half * 8 + place

    def dec_half():
        block = xv.at[slot_here, core]
        return remote(block, block, xx_send.at[0], xx_recv.at[0], x_half)

    def dec_z(part, way, step):
        half = x_hi if part == 0 else 1 - x_hi
        place = lax.rem(z + (NZ - step if way == 0 else step), NZ)
        groups = pl.ds(0, GROUPS)
        if step == 3:
            groups = pl.ds(way * (GROUPS // 2), GROUPS // 2)
        block = xv.at[dec_index(half, place), core, groups]
        return remote(
            block, block, xz_send.at[part, way, step], xz_recv.at[part, way, step],
            z_way[way],
        )

    def dec_share(part, slot):
        half = x_hi if part == 0 else 1 - x_hi
        shift = (NZ - 1, NZ - 2, NZ - 3, 1, 2, 3, 4, 0)[slot]
        block = xv.at[dec_index(half, lax.rem(z + shift, NZ)), core]
        return remote(
            block, block, xs_send.at[part, slot], xs_recv.at[part, slot], sibling
        )

    def partial_out(offset):
        return remote(
            dsend.at[lax.rem(grp + offset, GROUPS)], drecv.at[offset],
            d_send.at[offset], d_recv.at[offset], peer(offset),
        )

    def ring_block(way, step):
        if way == 0:
            return lax.rem(z + 4 - step, NZ)
        return lax.rem(z + 4 + step, NZ)

    def ring_rows(place):
        return pl.ds(aligned(place * CHIP, CHIP), CHIP)

    def ring_own(wave, way, part, step):
        return remote(
            pv.at[wave, ring_rows(ring_block(way, step)), pl.ds(part * LANE, LANE)],
            rv.at[wave, way, part, step],
            r_send.at[wave, way, part, step], r_recv.at[wave, way, part, step],
            z_way[way],
        )

    def ring_next(wave, way, part, step):
        return remote(
            rv.at[wave, way, part, step - 1], rv.at[wave, way, part, step],
            r_send.at[wave, way, part, step], r_recv.at[wave, way, part, step],
            z_way[way],
        )

    def ring_wait(wave, way, part, step):
        block = rv.at[wave, way, part, step]
        pltpu.make_async_copy(block, block, r_recv.at[wave, way, part, step]).wait()

    def chip_rows(which):
        return pl.ds(aligned(z * CHIP + which * OWN, 32), OWN)

    def grad_swap(wave):
        return remote(
            pv.at[wave, chip_rows(other), :], gx.at[wave],
            g_send.at[wave], g_recv.at[wave], sibling,
        )

    def home_half():
        return remote(
            pv.at[0, ring_rows(z), :], hx, h_send.at[0], h_recv.at[0], x_half
        )

    def state_cols(wave, half):
        return pl.ds(aligned(half * COLS + wave * WCOL, WCOL), WCOL)

    def store_out(wave, half, which):
        cols = state_cols(wave, half)
        target = (master_out, one_out, two_out)[which]
        return pltpu.make_async_copy(
            st.at[which, :, cols], target.at[:, cols], out_sem.at[wave, half, which]
        )

    pl.semaphore_wait(barrier, len(partners) + GROUPS - 1 + GROUPS - keeps_one)
    for piece in range(PIECES):
        cot_cross(piece).start()
    for index in range(4):
        for which in range(2):
            stays = dec_target(index, which) == shard
            pl.when(jnp.logical_not(stays))(lambda: dec_away(index, which).start())
            pl.when(stays)(lambda: dec_here(index, which).start())
    hid_sibling().start()
    cotx_sibling().start()
    cot_sibling().start()

    def dec_begin():
        for bucket in range(GROUPS):
            part = a2.at[bucket]
            pltpu.make_async_copy(part, part, a_recv.at[bucket]).wait()
        for offset in range(1, GROUPS):
            target = lax.rem(grp + offset, GROUPS)
            pick[target] = a2[held[target]]
            dec_pick(offset).start()
        xv[slot_here, core, grp] = a2[held[grp]]

    def dec_own():
        for offset in range(1, GROUPS):
            dec_pick(offset).wait_recv()
        dec_half().start()
        for way in range(2):
            dec_z(0, way, 0).start()
        dec_share(0, 7).start()

    def dec_first():
        dec_half().wait_recv()
        for way in range(2):
            dec_z(1, way, 0).start()
        dec_share(1, 7).start()

    def dec_step(step):
        for part in range(2):
            for way in range(2):
                dec_z(part, way, step).wait_recv()
                dec_z(part, way, step + 1).start()
                dec_share(part, way * 3 + step).start()

    def dec_last():
        for part in range(2):
            for way in range(2):
                dec_z(part, way, 3).wait_recv()
            dec_share(part, 6).start()

    def cot_near(piece):
        for way in range(2):
            cot_y(way, piece).wait_recv()
            cot_forward(way, piece).start()
            cot_share(1 + way, piece).start()

    def cot_far(piece):
        for way in range(2):
            cot_forward(way, piece).wait_recv()
        cot_share(3, piece).start()

    def cot_begin(piece):
        cot_cross(piece).wait_recv()
        for way in range(2):
            cot_y(way, piece).start()
        cot_share(0, piece).start()

    def hid_begin(wave):
        for target in range(2):
            hid_half(wave, target).start()

    acc[...] = jnp.zeros_like(acc)
    cot_begin(0)
    loads[1].wait()
    loads[5].wait()
    hid_sibling().wait_recv()
    cotx_sibling().wait_recv()

    def multiply(ring, rows, left, cols):
        def tile(index, carry):
            part = pl.ds(aligned(index * PCOL, PCOL), PCOL)
            value = lax.dot_general(
                left[rows, part], hidv[rows, cols],
                (((0,), (0,)), ((), ())), preferred_element_type=jnp.float32,
            )
            pv[ring, part, :] = value.astype(jnp.bfloat16)
            return carry

        lax.fori_loop(0, PIECES, tile, 0)
        for way in range(2):
            ring_own(ring, way, way, 0).start()
        for way in range(2):
            ring_own(ring, way, 1 - way, 1).start()

    def stage_sum(ring):
        pl.when(ring == 0)(
            lambda: multiply(0, slice(0, 2 * TOK), cotx, slice(0, WCOL))
        )

        @pl.when(ring == 1)
        def _():
            loads[0].wait()
            cot_sibling().wait_recv()
            multiply(1, slice(0, 2 * TOK), cotv, slice(0, WCOL))

        @pl.when(ring > 1)
        def _():
            for source in range(2):
                hid_half_wait(ring - 1, source)
            multiply(ring, slice(0, 4 * TOK), cotv, wave_cols(ring - 1))

    def ring_add(wave, way, part, step):
        ring_wait(wave, way, part, step - 1)
        own = pv[wave, ring_rows(ring_block(way, step)), part * LANE:(part + 1) * LANE]
        total = rv[wave, way, part, step - 1].astype(jnp.float32) + own.astype(jnp.float32)
        rv[wave, way, part, step - 1] = total.astype(jnp.bfloat16)
        ring_next(wave, way, part, step).start()

    def stage_near(wave):
        for way in range(2):
            ring_add(wave, way, way, 1)

    def stage_ring(wave, step):
        for part in range(2):
            for way in range(2):
                ring_add(wave, way, part, step)

    def home_sum(ring):
        for part in range(2):
            for way in range(2):
                ring_wait(ring, way, part, 3)
            lanes = slice(part * LANE, (part + 1) * LANE)
            total = pv[ring, ring_rows(z), lanes].astype(jnp.float32)
            for way in range(2):
                total = total + rv[ring, way, part, 3].astype(jnp.float32)
            pv[ring, ring_rows(z), lanes] = total.astype(jnp.bfloat16)

    def stage_home(ring):
        home_sum(ring)
        pl.when(ring == 0)(lambda: home_half().start())

        @pl.when(ring == 1)
        def _():
            home_half().wait_recv()
            total = pv[1, ring_rows(z), :].astype(jnp.float32) + hx[...].astype(jnp.float32)
            pv[1, ring_rows(z), :] = total.astype(jnp.bfloat16)

        pl.when(ring > 0)(lambda: grad_swap(ring).start())

    def adamw(wave, half, gradient):
        cols = state_cols(wave, half)
        master_now = st[0, :, cols]
        one = beta_one * st[1, :, cols] + (1.0 - beta_one) * gradient
        two = beta_two * st[2, :, cols] + (1.0 - beta_two) * gradient * gradient
        update = one / correct_one / (jnp.sqrt(two / correct_two) + epsilon)
        fresh = master_now - learn_rate * (update + decay_rate * master_now)
        st[0, :, cols] = fresh
        st[1, :, cols] = one
        st[2, :, cols] = two
        for which in range(3):
            store_out(wave, half, which).start()
        wv[half, :, wave_cols(wave)] = fresh.astype(jnp.bfloat16)

    def decode(wave):
        for half in range(2):
            first = half * (SLICES // 2) + 2 * wave
            for which in range(2):
                inputs = jnp.concatenate(
                    [
                        xv[first + part, which].reshape(GROUPS * HROWS, 128)
                        for part in range(2)
                    ],
                    axis=1,
                )
                acc[which] += lax.dot_general(
                    inputs, wv[half, :, wave_cols(wave)], (((1,), (1,)), ((), ())),
                    preferred_element_type=jnp.float32,
                )

    def stage_update(ring):
        wave = ring - 1
        adamw(wave, core, pv[ring, chip_rows(core), :].astype(jnp.float32))
        grad_swap(ring).wait_recv()
        adamw(wave, other, gx[ring].astype(jnp.float32))
        pl.when(ring > 1)(lambda: decode(wave))

    def tick(now, carry):
        @pl.when(now == 0)
        def _():
            cot_begin(1)
            dec_begin()

        @pl.when(now == 1)
        def _():
            cot_begin(2)
            cot_begin(3)
            dec_own()

        @pl.when(now == 2)
        def _():
            cot_near(0)
            cot_near(1)
            dec_first()

        @pl.when(now == 3)
        def _():
            cot_far(0)
            cot_near(2)
            hid_begin(1)
            cot_near(3)
            cot_far(1)

        @pl.when(now == 4)
        def _():
            cot_far(2)
            cot_far(3)
            hid_begin(2)
            dec_step(0)

        @pl.when(now == 5)
        def _():
            hid_begin(3)
            for which in range(3):
                loads[2 + which].wait()
            for which in range(4):
                for piece in range(PIECES):
                    cot_share(which, piece).wait_recv()

        pl.when(now == 6)(lambda: dec_step(1))
        pl.when(now == 8)(lambda: dec_step(2))
        pl.when(now == 9)(dec_last)

        @pl.when(now == 10)
        def _():
            for part in range(2):
                for slot in range(8):
                    dec_share(part, slot).wait_recv()
            decode(0)

        def each(ring, inner):
            stage = now - jnp.where(ring < 2, ring, 2 * ring + 1)
            home = jnp.where(ring == 1, 6, 4)
            pl.when(stage == 0)(lambda: stage_sum(ring))
            pl.when(stage == 1)(lambda: stage_near(ring))
            pl.when(jnp.logical_or(stage == 2, stage == 3))(
                lambda: stage_ring(ring, stage)
            )
            pl.when(stage == home)(lambda: stage_home(ring))
            pl.when(jnp.logical_and(stage == home + 1, ring > 0))(
                lambda: stage_update(ring)
            )
            return inner

        return lax.fori_loop(0, RINGS, each, carry)

    lax.fori_loop(0, LAST + 1, tick, 0)

    def own_rows(group):
        rows = pl.ds(aligned(group * HROWS, HROWS), HROWS)
        return acc[0, rows, :], acc[1, rows, :]

    for offset in range(1, GROUPS):
        group = lax.rem(grp + offset, GROUPS)
        dsend[group] = jnp.concatenate(own_rows(group), axis=0).T.astype(jnp.bfloat16)
        partial_out(offset).start()
    total = jnp.concatenate(own_rows(grp), axis=0).T
    for offset in range(1, GROUPS):
        partial_out(offset).wait_recv()
        total = total + drecv[offset].astype(jnp.float32)
    dec_out[...] = total.astype(jnp.bfloat16)

    cot_sibling().wait_send()
    cotx_sibling().wait_send()
    home_half().wait_send()
    hid_sibling().wait_send()
    dec_half().wait_send()
    for index in range(4):
        for which in range(2):
            stays = dec_target(index, which) == shard
            pl.when(jnp.logical_not(stays))(lambda: dec_away(index, which).wait_send())
    for offset in range(1, GROUPS):
        dec_pick(offset).wait_send()
        partial_out(offset).wait_send()
    for piece in range(PIECES):
        cot_cross(piece).wait_send()
        for way in range(2):
            cot_y(way, piece).wait_send()
            cot_forward(way, piece).wait_send()
        for which in range(4):
            cot_share(which, piece).wait_send()
    for part in range(2):
        for way in range(2):
            for step in range(4):
                dec_z(part, way, step).wait_send()
        for slot in range(8):
            dec_share(part, slot).wait_send()

    def drain(ring, carry):
        for way in range(2):
            for part in range(2):
                for step in range(0 if way == part else 1, 4):
                    ring_own(ring, way, part, step).wait_send()

        @pl.when(ring > 0)
        def _():
            grad_swap(ring).wait_send()
            for half in range(2):
                for which in range(3):
                    store_out(ring - 1, half, which).wait()

        @pl.when(ring > 1)
        def _():
            for target in range(2):
                hid_half(ring - 1, target).wait_send()

        return carry

    lax.fori_loop(0, RINGS, drain, 0)


def body(hidden_acts, cotangent, master, moment_one, moment_two, held_bucket, decode_in):
    any_spec = pl.BlockSpec(memory_space=pl.ANY)
    vmem = pltpu.VMEM
    sems = pltpu.SemaphoreType.DMA
    bf16, f32 = jnp.bfloat16, jnp.float32
    state = jax.ShapeDtypeStruct((OWN, BUCKET), f32)
    pairs = [
        (3,), (PIECES,), (2, PIECES), (2, PIECES), (4, PIECES), (WAVES, 2), (1,),
        (2, 2, 4), (2, 8), (RINGS, 2, 2, 4), (RINGS,), (1,),
    ]
    both = [sems(shape) for shape in pairs for _ in range(2)]
    *states, decoded = pl.pallas_call(
        kernel,
        out_shape=(state, state, state, jax.ShapeDtypeStruct((OWN, ROWS), bf16)),
        in_specs=[any_spec] * 5 + [pl.BlockSpec(memory_space=pltpu.SMEM), any_spec],
        out_specs=(any_spec, any_spec, any_spec, pl.BlockSpec(memory_space=pltpu.VMEM)),
        scratch_shapes=[
            vmem((4 * TOK, HALF), bf16),
            vmem((2 * TOK, HALF), bf16),
            vmem((4 * TOK, COLS), bf16),
            vmem((RINGS, HALF, WCOL), bf16),
            vmem((RINGS, 2, 2, 4, CHIP, LANE), bf16),
            vmem((RINGS, OWN, WCOL), bf16),
            vmem((CHIP, WCOL), bf16),
            vmem((3, OWN, BUCKET), f32),
            vmem((2, OWN, COLS), bf16),
            vmem((GROUPS, HROWS, 128), bf16),
            vmem((GROUPS, HROWS, 128), bf16),
            vmem((SLICES, 2, GROUPS, HROWS, 128), bf16),
            vmem((2, GROUPS * HROWS, OWN), f32),
            vmem((GROUPS, OWN, ROWS), bf16),
            vmem((GROUPS, OWN, ROWS), bf16),
            sems((6,)),
            sems((GROUPS,)),
            *both,
            sems((4, 2)),
            *[sems((GROUPS,)) for _ in range(4)],
            sems((WAVES, 2, 3)),
        ],
        compiler_params=pltpu.CompilerParams(
            collective_id=0, has_side_effects=True, vmem_limit_bytes=58 * 2**20
        ),
        cost_estimate=pl.CostEstimate(
            flops=12_000_000_000, bytes_accessed=30_000_000, transcendentals=0
        ),
    )(hidden_acts, cotangent, master, moment_one, moment_two, held_bucket, decode_in)
    return (*states, decoded.T)


def solution(mesh):
    placed = (
        P("shard", "grp"),
        P("shard", None),
        P("shard", "grp"),
        P("shard", "grp"),
        P("shard", "grp"),
        P(),
        P("grp", "shard"),
    )
    return jax.shard_map(
        body,
        mesh=mesh,
        in_specs=placed,
        out_specs=(P("shard", "grp"), P("shard", "grp"), P("shard", "grp"), P("grp", "shard")),
        check_vma=False,
    )
```

time: 168 us -> 136 us (0.81)
  Pallas kernels: 159 us -> 127 us
    pallas_call x1, Pallas kernels: 159 us -> 127 us  [body(): pl.pallas_call(kernel, out_shape=(state, state, state, jax.ShapeDtypeStru...]
    unnamed x7 -> x10, local copies, waits for them, and re-layouts: 5.45 us -> 6.07 us
where the time goes in v2:
time: 136 us; the launch traced here: 133 us
  Pallas kernels  127 us (93%)
  local copies, waits for them, and re-layouts  6.07 us (4%)
    pallas_call x1, Pallas kernels, body(): pl.pallas_call(kernel, out_shape=(state, state, state, jax.ShapeDtypeStru...  127 us
    unnamed x10, local copies, waits for them, and re-layouts  6.07 us

profile of v2, /device:TPU:24, one launch (start us, length us, event | category | flops | bytes accessed | tf_op | source)
XLA Modules:
  0.0 133.4 jit_solution(8313779777443993812)
XLA Ops:
  0.6 126.7 %shard_map.102 = (f32[160,2048]{1,0:T(8,128)}, f32[160,2048]{1,0:T(8,128)}, f32[160,2048]{1,0:T(8,128)}, bf16[160,128]{1,0:T(8,128)(2,1)}) custom-call(bf16[512,2048]{1,0:T(8,128)(2,1)} %hid.1, bf16[512,5120]{1,0:T(8,128)(2,1)} %cot.1, f32[160,2048]{1,0:T(8,128)} %master.1, f32[160,2048]{1,0:T(8,128)} %mom_one.1, f32[160,2048]{1,0:T(8,128)} %mom_two.1, ...), custom_call_target="tpu_custom_call" | custom-call | flops 12000000000 | bytes 30000000 | tf_op jit(solution)/shard_map/pallas_call | solution.py:638
  127.3 0.0 copy-start.1
  127.4 2.6 %copy.15 = f32[160,2048]{1,0:T(8,128)} copy(f32[160,2048]{1,0:T(8,128)} %get-tuple-element.16) | data formatting | bytes 2621440
  130.0 0.0 copy-done.1
  130.0 0.0 copy-start
  130.0 1.1 copy.16
  131.0 0.7 copy-done
  131.7 0.0 copy-start.2
  131.7 1.1 copy.17
  132.8 0.0 copy-done.2
  132.8 0.6 copy.18
Async XLA Ops:
  127.3 2.6 %copy-start.1 = (f32[160,2048]{1,0:T(8,128)S(1)}, f32[160,2048]{1,0:T(8,128)}, u32[]{:S(2)}) copy-start(f32[160,2048]{1,0:T(8,128)} %get-tuple-element.17) | copy-start | bytes 3932164
  130.0 1.8 %copy-start = (f32[160,2048]{1,0:T(8,128)S(1)}, f32[160,2048]{1,0:T(8,128)}, u32[]{:S(2)}) copy-start(f32[160,2048]{1,0:T(8,128)} %get-tuple-element.18) | copy-start | bytes 3932164
  131.7 1.1 copy-start.2

commit v3 on v2

--- a/solution.py
+++ b/solution.py
@@ -30,7 +30,8 @@
 ROWS = 128
 DCOL = 512
 RINGS = WAVES + 1
-LAST = 14
+START = (0, 1, 3, 4, 5)
+LAST = START[-1] + 5
 GROUPS = 8
 HROWS = ROWS // 2
 SLICES = 16
@@ -51,11 +52,11 @@
 def kernel(
     hid, cot, master, mom_one, mom_two, held, dec,
     master_out, one_out, two_out, dec_out,
-    cotv, cotx, hidv, pv, rv, gx, hx, st, wv, a2, pick, xv, acc, dsend, drecv,
+    cotv, cotx, hidv, pv, rv, gx, hx, wv, a2, pick, xv, acc, dsend, drecv,
     local_sem, a_recv, in_send, in_recv,
     cc_send, cc_recv, cy_send, cy_recv, cf_send, cf_recv, cs_send, cs_recv,
     hx_send, hx_recv, xx_send, xx_recv, xz_send, xz_recv, xs_send, xs_recv,
-    r_send, r_recv, g_send, g_recv, h_send, h_recv, a_send, p_send, p_recv, d_send, d_recv, out_sem,
+    r_send, r_recv, g_send, g_recv, h_send, h_recv, a_send, p_send, p_recv, d_send, d_recv,
 ):
     grp = lax.axis_index("grp")
     shard = lax.axis_index("shard")
@@ -116,9 +117,9 @@
             hid.at[:, pl.ds(aligned(core * COLS, COLS), COLS)], hidv.at[mine, :],
             local_sem.at[1],
         ),
-        pltpu.make_async_copy(master, st.at[0], local_sem.at[2]),
-        pltpu.make_async_copy(mom_one, st.at[1], local_sem.at[3]),
-        pltpu.make_async_copy(mom_two, st.at[2], local_sem.at[4]),
+        pltpu.make_async_copy(master, master_out, local_sem.at[2]),
+        pltpu.make_async_copy(mom_one, one_out, local_sem.at[3]),
+        pltpu.make_async_copy(mom_two, two_out, local_sem.at[4]),
         pltpu.make_async_copy(
             cot.at[:, pl.ds(aligned((1 - x_hi) * HALF, HALF), HALF)], cotx.at[mine, :],
             local_sem.at[5],
@@ -224,26 +225,27 @@
     def dec_index(half, place):
         return half * 8 + place
 
-    def dec_half():
-        block = xv.at[slot_here, core]
-        return remote(block, block, xx_send.at[0], xx_recv.at[0], x_half)
-
-    def dec_z(part, way, step):
-        half = x_hi if part == 0 else 1 - x_hi
+    def dec_place(slot):
+        shift = (NZ - 1, NZ - 2, NZ - 3, 1, 2, 3, 4, 0)[slot]
+        return lax.rem(z + shift, NZ)
+
+    def dec_half(slot):
+        block = xv.at[dec_index(x_hi, dec_place(slot)), core]
+        return remote(block, block, xx_send.at[slot], xx_recv.at[slot], x_half)
+
+    def dec_z(way, step):
         place = lax.rem(z + (NZ - step if way == 0 else step), NZ)
         groups = pl.ds(0, GROUPS)
         if step == 3:
             groups = pl.ds(way * (GROUPS // 2), GROUPS // 2)
-        block = xv.at[dec_index(half, place), core, groups]
-        return remote(
-            block, block, xz_send.at[part, way, step], xz_recv.at[part, way, step],
-            z_way[way],
+        block = xv.at[dec_index(x_hi, place), core, groups]
+        return remote(
+            block, block, xz_send.at[way, step], xz_recv.at[way, step], z_way[way]
         )
 
     def dec_share(part, slot):
         half = x_hi if part == 0 else 1 - x_hi
-        shift = (NZ - 1, NZ - 2, NZ - 3, 1, 2, 3, 4, 0)[slot]
-        block = xv.at[dec_index(half, lax.rem(z + shift, NZ)), core]
+        block = xv.at[dec_index(half, dec_place(slot)), core]
         return remote(
             block, block, xs_send.at[part, slot], xs_recv.at[part, slot], sibling
         )
@@ -297,13 +299,6 @@
 
     def state_cols(wave, half):
         return pl.ds(aligned(half * COLS + wave * WCOL, WCOL), WCOL)
-
-    def store_out(wave, half, which):
-        cols = state_cols(wave, half)
-        target = (master_out, one_out, two_out)[which]
-        return pltpu.make_async_copy(
-            st.at[which, :, cols], target.at[:, cols], out_sem.at[wave, half, which]
-        )
 
     pl.semaphore_wait(barrier, len(partners) + GROUPS - 1 + GROUPS - keeps_one)
     for piece in range(PIECES):
@@ -330,29 +325,28 @@
     def dec_own():
         for offset in range(1, GROUPS):
             dec_pick(offset).wait_recv()
-        dec_half().start()
-        for way in range(2):
-            dec_z(0, way, 0).start()
+        for way in range(2):
+            dec_z(way, 0).start()
+        dec_half(7).start()
         dec_share(0, 7).start()
 
-    def dec_first():
-        dec_half().wait_recv()
-        for way in range(2):
-            dec_z(1, way, 0).start()
-        dec_share(1, 7).start()
-
     def dec_step(step):
-        for part in range(2):
-            for way in range(2):
-                dec_z(part, way, step).wait_recv()
-                dec_z(part, way, step + 1).start()
-                dec_share(part, way * 3 + step).start()
+        for way in range(2):
+            dec_z(way, step).wait_recv()
+            dec_z(way, step + 1).start()
+            dec_half(way * 3 + step).start()
+            dec_share(0, way * 3 + step).start()
 
     def dec_last():
-        for part in range(2):
-            for way in range(2):
-                dec_z(part, way, 3).wait_recv()
-            dec_share(part, 6).start()
+        for way in range(2):
+            dec_z(way, 3).wait_recv()
+        dec_half(6).start()
+        dec_share(0, 6).start()
+
+    def dec_cross(*slots):
+        for slot in slots:
+            dec_half(slot).wait_recv()
+            dec_share(1, slot).start()
 
     def cot_near(piece):
         for way in range(2):
@@ -371,12 +365,27 @@
             cot_y(way, piece).start()
         cot_share(0, piece).start()
 
+    def cot_end():
+        for which in range(4):
+            for piece in range(PIECES):
+                cot_share(which, piece).wait_recv()
+
+    def state_end():
+        for which in range(3):
+            loads[2 + which].wait()
+
+    def dec_end():
+        for part in range(2):
+            for slot in range(8):
+                dec_share(part, slot).wait_recv()
+
     def hid_begin(wave):
         for target in range(2):
             hid_half(wave, target).start()
 
     acc[...] = jnp.zeros_like(acc)
     cot_begin(0)
+    cot_begin(1)
     loads[1].wait()
     loads[5].wait()
     hid_sibling().wait_recv()
@@ -455,16 +464,14 @@
 
     def adamw(wave, half, gradient):
         cols = state_cols(wave, half)
-        master_now = st[0, :, cols]
-        one = beta_one * st[1, :, cols] + (1.0 - beta_one) * gradient
-        two = beta_two * st[2, :, cols] + (1.0 - beta_two) * gradient * gradient
+        master_now = master_out[:, cols]
+        one = beta_one * one_out[:, cols] + (1.0 - beta_one) * gradient
+        two = beta_two * two_out[:, cols] + (1.0 - beta_two) * gradient * gradient
         update = one / correct_one / (jnp.sqrt(two / correct_two) + epsilon)
         fresh = master_now - learn_rate * (update + decay_rate * master_now)
-        st[0, :, cols] = fresh
-        st[1, :, cols] = one
-        st[2, :, cols] = two
-        for which in range(3):
-            store_out(wave, half, which).start()
+        master_out[:, cols] = fresh
+        one_out[:, cols] = one
+        two_out[:, cols] = two
         wv[half, :, wave_cols(wave)] = fresh.astype(jnp.bfloat16)
 
     def decode(wave):
@@ -488,63 +495,23 @@
         adamw(wave, core, pv[ring, chip_rows(core), :].astype(jnp.float32))
         grad_swap(ring).wait_recv()
         adamw(wave, other, gx[ring].astype(jnp.float32))
-        pl.when(ring > 1)(lambda: decode(wave))
 
     def tick(now, carry):
-        @pl.when(now == 0)
-        def _():
-            cot_begin(1)
-            dec_begin()
-
-        @pl.when(now == 1)
-        def _():
-            cot_begin(2)
-            cot_begin(3)
-            dec_own()
-
-        @pl.when(now == 2)
-        def _():
-            cot_near(0)
-            cot_near(1)
-            dec_first()
-
-        @pl.when(now == 3)
-        def _():
-            cot_far(0)
-            cot_near(2)
-            hid_begin(1)
-            cot_near(3)
-            cot_far(1)
-
-        @pl.when(now == 4)
-        def _():
-            cot_far(2)
-            cot_far(3)
-            hid_begin(2)
-            dec_step(0)
-
-        @pl.when(now == 5)
-        def _():
-            hid_begin(3)
-            for which in range(3):
-                loads[2 + which].wait()
-            for which in range(4):
-                for piece in range(PIECES):
-                    cot_share(which, piece).wait_recv()
-
-        pl.when(now == 6)(lambda: dec_step(1))
-        pl.when(now == 8)(lambda: dec_step(2))
-        pl.when(now == 9)(dec_last)
-
-        @pl.when(now == 10)
-        def _():
-            for part in range(2):
-                for slot in range(8):
-                    dec_share(part, slot).wait_recv()
-            decode(0)
+        def at(moment, *work):
+            @pl.when(now == moment)
+            def _():
+                for part in work:
+                    part()
+
+        at(2, lambda: cot_near(2), lambda: hid_begin(1))
+        at(3, lambda: cot_far(2), lambda: cot_far(3), cot_end, lambda: hid_begin(2))
+        at(7, state_end)
 
         def each(ring, inner):
-            stage = now - jnp.where(ring < 2, ring, 2 * ring + 1)
+            start = START[-1]
+            for index in range(RINGS - 1):
+                start = jnp.where(ring == index, START[index], start)
+            stage = now - start
             home = jnp.where(ring == 1, 6, 4)
             pl.when(stage == 0)(lambda: stage_sum(ring))
             pl.when(stage == 1)(lambda: stage_near(ring))
@@ -557,7 +524,18 @@
             )
             return inner
 
-        return lax.fori_loop(0, RINGS, each, carry)
+        lax.fori_loop(0, RINGS, each, 0)
+        at(0, lambda: cot_begin(2), lambda: cot_near(0), lambda: dec_begin())
+        at(1, lambda: cot_begin(3), lambda: cot_near(1), lambda: cot_far(0), lambda: dec_own())
+        at(2, lambda: cot_near(3), lambda: cot_far(1))
+        at(3, lambda: hid_begin(3), lambda: dec_step(0))
+        at(5, lambda: dec_step(1), lambda: dec_cross(7, 0, 3))
+        at(6, lambda: dec_step(2))
+        at(7, lambda: dec_last(), lambda: dec_cross(1, 4))
+        at(8, lambda: dec_cross(2, 5, 6))
+        at(9, lambda: dec_end(), lambda: decode(0), lambda: decode(1), lambda: decode(2))
+        at(10, lambda: decode(3))
+        return carry
 
     lax.fori_loop(0, LAST + 1, tick, 0)
 
@@ -569,24 +547,17 @@
         group = lax.rem(grp + offset, GROUPS)
         dsend[group] = jnp.concatenate(own_rows(group), axis=0).T.astype(jnp.bfloat16)
         partial_out(offset).start()
-    total = jnp.concatenate(own_rows(grp), axis=0).T
-    for offset in range(1, GROUPS):
-        partial_out(offset).wait_recv()
-        total = total + drecv[offset].astype(jnp.float32)
-    dec_out[...] = total.astype(jnp.bfloat16)
 
     cot_sibling().wait_send()
     cotx_sibling().wait_send()
     home_half().wait_send()
     hid_sibling().wait_send()
-    dec_half().wait_send()
     for index in range(4):
         for which in range(2):
             stays = dec_target(index, which) == shard
             pl.when(jnp.logical_not(stays))(lambda: dec_away(index, which).wait_send())
     for offset in range(1, GROUPS):
         dec_pick(offset).wait_send()
-        partial_out(offset).wait_send()
     for piece in range(PIECES):
         cot_cross(piece).wait_send()
         for way in range(2):
@@ -594,11 +565,12 @@
             cot_forward(way, piece).wait_send()
         for which in range(4):
             cot_share(which, piece).wait_send()
-    for part in range(2):
-        for way in range(2):
-            for step in range(4):
-                dec_z(part, way, step).wait_send()
-        for slot in range(8):
+    for way in range(2):
+        for step in range(4):
+            dec_z(way, step).wait_send()
+    for slot in range(8):
+        dec_half(slot).wait_send()
+        for part in range(2):
             dec_share(part, slot).wait_send()
 
     def drain(ring, carry):
@@ -610,9 +582,6 @@
         @pl.when(ring > 0)
         def _():
             grad_swap(ring).wait_send()
-            for half in range(2):
-                for which in range(3):
-                    store_out(ring - 1, half, which).wait()
 
         @pl.when(ring > 1)
         def _():
@@ -622,6 +591,14 @@
         return carry
 
     lax.fori_loop(0, RINGS, drain, 0)
+
+    total = jnp.concatenate(own_rows(grp), axis=0).T
+    for offset in range(1, GROUPS):
+        partial_out(offset).wait_recv()
+        total = total + drecv[offset].astype(jnp.float32)
+    dec_out[...] = total.astype(jnp.bfloat16)
+    for offset in range(1, GROUPS):
+        partial_out(offset).wait_send()
 
 
 def body(hidden_acts, cotangent, master, moment_one, moment_two, held_bucket, decode_in):
@@ -629,17 +606,16 @@
     vmem = pltpu.VMEM
     sems = pltpu.SemaphoreType.DMA
     bf16, f32 = jnp.bfloat16, jnp.float32
-    state = jax.ShapeDtypeStruct((OWN, BUCKET), f32)
     pairs = [
-        (3,), (PIECES,), (2, PIECES), (2, PIECES), (4, PIECES), (WAVES, 2), (1,),
-        (2, 2, 4), (2, 8), (RINGS, 2, 2, 4), (RINGS,), (1,),
+        (3,), (PIECES,), (2, PIECES), (2, PIECES), (4, PIECES), (WAVES, 2), (8,),
+        (2, 4), (2, 8), (RINGS, 2, 2, 4), (RINGS,), (1,),
     ]
     both = [sems(shape) for shape in pairs for _ in range(2)]
     *states, decoded = pl.pallas_call(
         kernel,
-        out_shape=(state, state, state, jax.ShapeDtypeStruct((OWN, ROWS), bf16)),
+        out_shape=(pltpu.VMEM((OWN, BUCKET), f32),) * 3 + (vmem((OWN, ROWS), bf16),),
         in_specs=[any_spec] * 5 + [pl.BlockSpec(memory_space=pltpu.SMEM), any_spec],
-        out_specs=(any_spec, any_spec, any_spec, pl.BlockSpec(memory_space=pltpu.VMEM)),
+        out_specs=(pl.BlockSpec(memory_space=pltpu.VMEM),) * 4,
         scratch_shapes=[
             vmem((4 * TOK, HALF), bf16),
             vmem((2 * TOK, HALF), bf16),
@@ -648,7 +624,6 @@
             vmem((RINGS, 2, 2, 4, CHIP, LANE), bf16),
             vmem((RINGS, OWN, WCOL), bf16),
             vmem((CHIP, WCOL), bf16),
-            vmem((3, OWN, BUCKET), f32),
             vmem((2, OWN, COLS), bf16),
             vmem((GROUPS, HROWS, 128), bf16),
             vmem((GROUPS, HROWS, 128), bf16),
@@ -661,7 +636,6 @@
             *both,
             sems((4, 2)),
             *[sems((GROUPS,)) for _ in range(4)],
-            sems((WAVES, 2, 3)),
         ],
         compiler_params=pltpu.CompilerParams(
             collective_id=0, has_side_effects=True, vmem_limit_bytes=58 * 2**20

time: 136 us -> 121 us (0.89); the launches traced: 133 us -> 121 us
  Pallas kernels: 127 us -> 117 us
  local copies, waits for them, and re-layouts: 6.07 us -> 3.79 us
    pallas_call x1, Pallas kernels: 127 us -> 117 us  [body(): pl.pallas_call(kernel, out_shape=(pltpu.VMEM((OWN, BUCKET), f32),) * 3 +...]
    unnamed x10 -> x4, local copies, waits for them, and re-layouts: 6.07 us -> 3.79 us
where the time goes in v3:
time: 121 us
  Pallas kernels  117 us (97%)
  local copies, waits for them, and re-layouts  3.79 us (3%)
    pallas_call x1, Pallas kernels, body(): pl.pallas_call(kernel, out_shape=(pltpu.VMEM((OWN, BUCKET), f32),) * 3 +...  117 us
    unnamed x4, local copies, waits for them, and re-layouts  3.79 us

profile of v3, /device:TPU:24, one launch (start us, length us, event | category | flops | bytes accessed | tf_op | source)
XLA Modules:
  0.0 121.1 jit_solution(7752705288060025198)
XLA Ops:
  0.6 116.7 %shard_map.102 = (f32[160,2048]{1,0:T(8,128)S(1)}, f32[160,2048]{1,0:T(8,128)S(1)}, f32[160,2048]{1,0:T(8,128)S(1)}, bf16[160,128]{1,0:T(8,128)(2,1)S(1)}) custom-call(bf16[512,2048]{1,0:T(8,128)(2,1)} %hid.1, bf16[512,5120]{1,0:T(8,128)(2,1)} %cot.1, f32[160,2048]{1,0:T(8,128)} %master.1, f32[160,2048]{1,0:T(8,128)} %mom_one.1, f32[160,2048]{1,0:T(8,128)} %mom_two.1, ...), custom_call_target="tpu_custom_call" | custom-call | flops 12000000000 | bytes 30000000 | tf_op jit(solution)/shard_map/pallas_call | solution.py:614
  117.3 1.1 copy.15
  118.4 0.6 copy.18
  119.0 1.1 copy.16
  120.0 1.1 copy.17

commit v4 on v3

--- a/solution.py
+++ b/solution.py
@@ -125,8 +125,8 @@
             local_sem.at[5],
         ),
     ]
-    for copy in loads:
-        copy.start()
+    for index in (1, 5, 0):
+        loads[index].start()
 
     def cot_sibling():
         return remote(
@@ -175,12 +175,9 @@
             part, part, cf_send.at[way, piece], cf_recv.at[way, piece], y_way[way]
         )
 
-    def cot_share(which, piece):
-        owner = lax.rem(y + (0, NY - 1, 1, 2)[which], NY)
-        part = cotv.at[cot_rows(owner, 0, PROW), cot_cols(piece)]
-        return remote(
-            part, part, cs_send.at[which, piece], cs_recv.at[which, piece], sibling
-        )
+    def cot_share(piece):
+        part = cotv.at[cot_rows(0, 0, TOK), cot_cols(piece)]
+        return remote(part, part, cs_send.at[piece], cs_recv.at[piece], sibling)
 
     def wave_cols(wave):
         return pl.ds(aligned(wave * WCOL, WCOL), WCOL)
@@ -243,12 +240,10 @@
             block, block, xz_send.at[way, step], xz_recv.at[way, step], z_way[way]
         )
 
-    def dec_share(part, slot):
+    def dec_share(part):
         half = x_hi if part == 0 else 1 - x_hi
-        block = xv.at[dec_index(half, dec_place(slot)), core]
-        return remote(
-            block, block, xs_send.at[part, slot], xs_recv.at[part, slot], sibling
-        )
+        block = xv.at[pl.ds(half * 8, 8), core]
+        return remote(block, block, xs_send.at[part], xs_recv.at[part], sibling)
 
     def partial_out(offset):
         return remote(
@@ -328,47 +323,45 @@
         for way in range(2):
             dec_z(way, 0).start()
         dec_half(7).start()
-        dec_share(0, 7).start()
 
     def dec_step(step):
         for way in range(2):
             dec_z(way, step).wait_recv()
             dec_z(way, step + 1).start()
             dec_half(way * 3 + step).start()
-            dec_share(0, way * 3 + step).start()
 
     def dec_last():
         for way in range(2):
             dec_z(way, 3).wait_recv()
         dec_half(6).start()
-        dec_share(0, 6).start()
+        dec_share(0).start()
 
     def dec_cross(*slots):
         for slot in slots:
             dec_half(slot).wait_recv()
-            dec_share(1, slot).start()
 
     def cot_near(piece):
         for way in range(2):
             cot_y(way, piece).wait_recv()
             cot_forward(way, piece).start()
-            cot_share(1 + way, piece).start()
 
     def cot_far(piece):
         for way in range(2):
             cot_forward(way, piece).wait_recv()
-        cot_share(3, piece).start()
+        cot_share(piece).start()
 
     def cot_begin(piece):
         cot_cross(piece).wait_recv()
         for way in range(2):
             cot_y(way, piece).start()
-        cot_share(0, piece).start()
 
     def cot_end():
-        for which in range(4):
-            for piece in range(PIECES):
-                cot_share(which, piece).wait_recv()
+        for piece in range(PIECES):
+            cot_share(piece).wait_recv()
+
+    def state_begin():
+        for which in range(3):
+            loads[2 + which].start()
 
     def state_end():
         for which in range(3):
@@ -376,8 +369,7 @@
 
     def dec_end():
         for part in range(2):
-            for slot in range(8):
-                dec_share(part, slot).wait_recv()
+            dec_share(part).wait_recv()
 
     def hid_begin(wave):
         for target in range(2):
@@ -508,36 +500,35 @@
         at(7, state_end)
 
         def each(ring, inner):
-            start = START[-1]
-            for index in range(RINGS - 1):
-                start = jnp.where(ring == index, START[index], start)
-            stage = now - start
-            home = jnp.where(ring == 1, 6, 4)
+            stage = now - START[ring]
+            home = (6 if ring == 1 else 4)
             pl.when(stage == 0)(lambda: stage_sum(ring))
             pl.when(stage == 1)(lambda: stage_near(ring))
-            pl.when(jnp.logical_or(stage == 2, stage == 3))(
+            pl.when(stage in (2, 3))(
                 lambda: stage_ring(ring, stage)
             )
             pl.when(stage == home)(lambda: stage_home(ring))
-            pl.when(jnp.logical_and(stage == home + 1, ring > 0))(
+            pl.when(stage == home + 1 and ring > 0)(
                 lambda: stage_update(ring)
             )
             return inner
 
-        lax.fori_loop(0, RINGS, each, 0)
+        for ring in range(RINGS):
+            each(ring, 0)
         at(0, lambda: cot_begin(2), lambda: cot_near(0), lambda: dec_begin())
         at(1, lambda: cot_begin(3), lambda: cot_near(1), lambda: cot_far(0), lambda: dec_own())
-        at(2, lambda: cot_near(3), lambda: cot_far(1))
+        at(2, lambda: cot_near(3), lambda: cot_far(1), state_begin)
         at(3, lambda: hid_begin(3), lambda: dec_step(0))
         at(5, lambda: dec_step(1), lambda: dec_cross(7, 0, 3))
         at(6, lambda: dec_step(2))
         at(7, lambda: dec_last(), lambda: dec_cross(1, 4))
-        at(8, lambda: dec_cross(2, 5, 6))
+        at(8, lambda: dec_cross(2, 5, 6), lambda: dec_share(1).start())
         at(9, lambda: dec_end(), lambda: decode(0), lambda: decode(1), lambda: decode(2))
         at(10, lambda: decode(3))
         return carry
 
-    lax.fori_loop(0, LAST + 1, tick, 0)
+    for now in range(LAST + 1):
+        tick(now, 0)
 
     def own_rows(group):
         rows = pl.ds(aligned(group * HROWS, HROWS), HROWS)
@@ -563,15 +554,14 @@
         for way in range(2):
             cot_y(way, piece).wait_send()
             cot_forward(way, piece).wait_send()
-        for which in range(4):
-            cot_share(which, piece).wait_send()
+        cot_share(piece).wait_send()
     for way in range(2):
         for step in range(4):
             dec_z(way, step).wait_send()
     for slot in range(8):
         dec_half(slot).wait_send()
-        for part in range(2):
-            dec_share(part, slot).wait_send()
+    for part in range(2):
+        dec_share(part).wait_send()
 
     def drain(ring, carry):
         for way in range(2):
@@ -607,8 +597,8 @@
     sems = pltpu.SemaphoreType.DMA
     bf16, f32 = jnp.bfloat16, jnp.float32
     pairs = [
-        (3,), (PIECES,), (2, PIECES), (2, PIECES), (4, PIECES), (WAVES, 2), (8,),
-        (2, 4), (2, 8), (RINGS, 2, 2, 4), (RINGS,), (1,),
+        (3,), (PIECES,), (2, PIECES), (2, PIECES), (PIECES,), (WAVES, 2), (8,),
+        (2, 4), (2,), (RINGS, 2, 2, 4), (RINGS,), (1,),
     ]
     both = [sems(shape) for shape in pairs for _ in range(2)]
     *states, decoded = pl.pallas_call(

time: 121 us -> 120 us (level)
  no operation moved by 1% of the time
where the time goes in v4:
time: 120 us
  Pallas kernels  116 us (97%)
  local copies, waits for them, and re-layouts  3.79 us (3%)
    pallas_call x1, Pallas kernels, body(): pl.pallas_call(kernel, out_shape=(pltpu.VMEM((OWN, BUCKET), f32),) * 3 +...  116 us
    unnamed x4, local copies, waits for them, and re-layouts  3.79 us

profile of v4, /device:TPU:24, one launch (start us, length us, event | category | flops | bytes accessed | tf_op | source)
XLA Modules:
  0.0 120.0 jit_solution(8851848183993244189)
XLA Ops:
  0.6 115.5 %shard_map.102 = (f32[160,2048]{1,0:T(8,128)S(1)}, f32[160,2048]{1,0:T(8,128)S(1)}, f32[160,2048]{1,0:T(8,128)S(1)}, bf16[160,128]{1,0:T(8,128)(2,1)S(1)}) custom-call(bf16[512,2048]{1,0:T(8,128)(2,1)} %hid.1, bf16[512,5120]{1,0:T(8,128)(2,1)} %cot.1, f32[160,2048]{1,0:T(8,128)} %master.1, f32[160,2048]{1,0:T(8,128)} %mom_one.1, f32[160,2048]{1,0:T(8,128)} %mom_two.1, ...), custom_call_target="tpu_custom_call" | custom-call | flops 12000000000 | bytes 30000000 | tf_op jit(solution)/shard_map/pallas_call | solution.py:604
  116.2 1.1 copy.15
  117.2 0.6 copy.18
  117.8 1.1 copy.16
  118.9 1.1 copy.17

commit v5 on v4

--- a/solution.py
+++ b/solution.py
@@ -459,15 +459,15 @@
         master_now = master_out[:, cols]
         one = beta_one * one_out[:, cols] + (1.0 - beta_one) * gradient
         two = beta_two * two_out[:, cols] + (1.0 - beta_two) * gradient * gradient
-        update = one / correct_one / (jnp.sqrt(two / correct_two) + epsilon)
+        update = one * (1.0 / correct_one) / (jnp.sqrt(two * (1.0 / correct_two)) + epsilon)
         fresh = master_now - learn_rate * (update + decay_rate * master_now)
         master_out[:, cols] = fresh
         one_out[:, cols] = one
         two_out[:, cols] = two
         wv[half, :, wave_cols(wave)] = fresh.astype(jnp.bfloat16)
 
-    def decode(wave):
-        for half in range(2):
+    def decode(wave, halves=(0, 1)):
+        for half in halves:
             first = half * (SLICES // 2) + 2 * wave
             for which in range(2):
                 inputs = jnp.concatenate(
@@ -485,8 +485,12 @@
     def stage_update(ring):
         wave = ring - 1
         adamw(wave, core, pv[ring, chip_rows(core), :].astype(jnp.float32))
+        if ring == RINGS - 1:
+            decode(wave, (core,))
         grad_swap(ring).wait_recv()
         adamw(wave, other, gx[ring].astype(jnp.float32))
+        if ring == RINGS - 1:
+            decode(wave, (other,))
 
     def tick(now, carry):
         def at(moment, *work):
@@ -515,16 +519,16 @@
 
         for ring in range(RINGS):
             each(ring, 0)
-        at(0, lambda: cot_begin(2), lambda: cot_near(0), lambda: dec_begin())
-        at(1, lambda: cot_begin(3), lambda: cot_near(1), lambda: cot_far(0), lambda: dec_own())
+        at(0, lambda: cot_begin(2), lambda: cot_near(0))
+        at(1, lambda: cot_begin(3), lambda: cot_near(1), lambda: cot_far(0), dec_begin)
         at(2, lambda: cot_near(3), lambda: cot_far(1), state_begin)
-        at(3, lambda: hid_begin(3), lambda: dec_step(0))
-        at(5, lambda: dec_step(1), lambda: dec_cross(7, 0, 3))
-        at(6, lambda: dec_step(2))
+        at(3, lambda: hid_begin(3), dec_own)
+        at(4, lambda: dec_step(0))
+        at(5, lambda: dec_step(1))
+        at(6, lambda: dec_step(2), lambda: dec_cross(7, 0, 3))
         at(7, lambda: dec_last(), lambda: dec_cross(1, 4))
         at(8, lambda: dec_cross(2, 5, 6), lambda: dec_share(1).start())
         at(9, lambda: dec_end(), lambda: decode(0), lambda: decode(1), lambda: decode(2))
-        at(10, lambda: decode(3))
         return carry
 
     for now in range(LAST + 1):

time: 120 us -> 120 us (level); the launches traced: 120 us -> 119 us
  Pallas kernels: 116 us -> 114 us
    pallas_call x1, Pallas kernels: 116 us -> 114 us  [body(): pl.pallas_call(kernel, out_shape=(pltpu.VMEM((OWN, BUCKET), f32),) * 3 +...]
where the time goes in v5:
time: 120 us; the launch traced here: 119 us
  Pallas kernels  114 us (95%)
  local copies, waits for them, and re-layouts  3.79 us (3%)
    pallas_call x1, Pallas kernels, body(): pl.pallas_call(kernel, out_shape=(pltpu.VMEM((OWN, BUCKET), f32),) * 3 +...  114 us
    unnamed x4, local copies, waits for them, and re-layouts  3.79 us

profile of v5, /device:TPU:24, one launch (start us, length us, event | category | flops | bytes accessed | tf_op | source)
XLA Modules:
  0.0 118.6 jit_solution(15235080396738168155)
XLA Ops:
  0.6 114.2 %shard_map.102 = (f32[160,2048]{1,0:T(8,128)S(1)}, f32[160,2048]{1,0:T(8,128)S(1)}, f32[160,2048]{1,0:T(8,128)S(1)}, bf16[160,128]{1,0:T(8,128)(2,1)S(1)}) custom-call(bf16[512,2048]{1,0:T(8,128)(2,1)} %hid.1, bf16[512,5120]{1,0:T(8,128)(2,1)} %cot.1, f32[160,2048]{1,0:T(8,128)} %master.1, f32[160,2048]{1,0:T(8,128)} %mom_one.1, f32[160,2048]{1,0:T(8,128)} %mom_two.1, ...), custom_call_target="tpu_custom_call" | custom-call | flops 12000000000 | bytes 30000000 | tf_op jit(solution)/shard_map/pallas_call | solution.py:608
  114.8 1.1 copy.15
  115.9 0.6 copy.18
  116.5 1.1 copy.16
  117.6 1.1 copy.17
